TPU v7x, 256 devices: a whole 4x4x8 slice. The times are simulated.
256 devices in a mesh: sub: 2 (over core), row: 8 (over y_lo, x), col: 16 (over z, y_hi).
Axes of the slice: x: 4, y: 4 (y_hi: 2, y_lo: 2; y = y_hi * 2 + y_lo), z: 8, core: 2. Of those that a mesh axis runs over, the one named last changes fastest.
Arguments:
- initial: float32 [12, 16, 256, 4096], P(None, ('sub', 'row'), None, 'col'), may hold values from -1 to 6
- pattern: int32 [12, 16, 16], P(None, ('sub', 'row'), 'col'), may hold values from 0 to 1, as said below
- rmap: int32 [2, 8, 16], replicated, may hold values from 0 to 191, as said below
- child_update: float32 [2, 8, 16, 256, 4096], P('sub', 'row', None, None, 'col'), may hold values from -0.5 to 0.5
Outputs:
- factored: float32 [12, 16, 256, 4096], P(None, ('sub', 'row'), None, 'col')
Inputs may be any that keep to these rules, and one draw needn't show every extreme that they name: Within one child the 128 entries are distinct tile rows; in each block rmap[c, r, :] exactly two remainders modulo 16 appear 2 times, two never, the others once. pattern[p, p] = 1 for p < 16.
All inputs are finite; a program needn't handle non-finite values.
Results may differ from a plain program's by a relative error of at most 0.0001.
Values sent between devices are 32-bit elements; how exact they have to be, the bound alone decides.
A program may use at most 128 MiB of HBM per device.

v0:
```python
import jax
import jax.numpy as jnp
from jax import lax
from jax.sharding import PartitionSpec as P

CAP = 2


def spread(block, axis, holder):
    block = jnp.where(lax.axis_index(axis) == holder, block, jnp.zeros_like(block))
    return lax.psum(block, axis)


def slot_ranks(tile_map, owners):
    target = tile_map % owners
    index = jnp.arange(target.shape[0])
    earlier = (target[None, :] == target[:, None]) & (index[None, :] < index[:, None])
    return (target, jnp.sum(earlier.astype(jnp.int32), axis=1))


def right_solve(factor, stacked):
    tile = factor.shape[0]
    flat = lax.linalg.triangular_solve(
        factor, stacked.reshape(-1, tile), left_side=False, lower=True, transpose_a=True
    )
    return flat.reshape(stacked.shape)


def per_device(initial, pattern, rmap, child_update):
    owners = lax.axis_size("sub") * lax.axis_size("row")
    frows = initial.shape[0]
    owner_me = lax.axis_index(("sub", "row"))
    child = lax.axis_index("sub")
    proc_row = lax.axis_index("row")
    column_me = lax.axis_index("col")
    slot_ids = jnp.arange(CAP)
    owner_ids = jnp.arange(owners)
    own_map = rmap[child, proc_row]
    target, ranks = slot_ranks(own_map, owners)
    select = (
        (target[None, None, :] == owner_ids[:, None, None])
        & (ranks[None, None, :] == slot_ids[None, :, None])
    ).astype(jnp.float32)
    outgoing = jnp.einsum(
        "dsk,kab->dsab", select, child_update[0, 0], precision=lax.Precision.HIGHEST
    )
    incoming = lax.all_to_all(outgoing, ("sub", "row"), split_axis=0, concat_axis=0, tiled=True)
    all_maps = rmap.reshape(owners, owners)
    all_target, all_ranks = jax.vmap(lambda one: slot_ranks(one, owners))(all_maps)
    local_row = all_maps // owners
    placing = (
        (all_target == owner_me)[None, :, None, :]
        & (all_ranks[None, :, None, :] == slot_ids[None, None, :, None])
        & (local_row[None, :, None, :] == jnp.arange(frows)[:, None, None, None])
    )
    placing = jnp.sum(placing.astype(jnp.float32), axis=3)
    front = initial[:, 0] * pattern[:, 0, :, None].astype(jnp.float32)
    front = front + jnp.einsum("msj,sjab->mab", placing, incoming, precision=lax.Precision.HIGHEST)
    tile_row = jnp.arange(frows) * owners + owner_me
    for step in range(2):
        column = spread(front, "col", step)
        diag = spread(column[step // owners], ("sub", "row"), step % owners)
        factor = jnp.linalg.cholesky(diag)
        solved = right_solve(factor, column)
        panel = jnp.where(
            (tile_row == step)[:, None, None],
            factor[None],
            jnp.where((tile_row > step)[:, None, None], solved, jnp.zeros_like(solved)),
        )
        own_tile = lax.dynamic_index_in_dim(panel, column_me // owners, 0, keepdims=False)
        row_tile = spread(own_tile, ("sub", "row"), column_me % owners)
        update = jnp.einsum("mab,cb->mac", panel, row_tile, precision=lax.Precision.HIGHEST)
        lower = (column_me > step) & (tile_row > step)[:, None, None]
        front = jnp.where(column_me == step, panel, jnp.where(lower, front - update, front))
    return front[:, None]


def solution(mesh):
    return jax.shard_map(
        per_device,
        mesh=mesh,
        in_specs=(
            P(None, ("sub", "row"), None, "col"),
            P(None, ("sub", "row"), "col"),
            P(),
            P("sub", "row", None, None, "col"),
        ),
        out_specs=P(None, ("sub", "row"), None, "col"),
        check_vma=False,
    )
```

profile of v0, /device:TPU:6, one launch (start us, length us, event | category | flops | bytes accessed | tf_op | source)
XLA Modules:
  0.0 1269.4 jit_solution(1868014286174128155)
XLA Ops:
  8.1 7.7 fusion.2
  15.9 9.7 copy.61
  25.6 6.7 all-to-all-start
  32.3 2.4 copy.59
  35.4 107.6 %all-to-all-done = f32[16,2,256,256]{3,1,2,0:T(2,128)} async-done(((f32[16,2,256,256]{3,1,2,0:T(2,128)}), f32[16,2,256,256]{3,1,2,0:T(2,128)}, u32[]{:S(2)}, u32[]{:S(2)}) %all-to-all-start) | async-done | bytes 8388640 | tf_op jit(solution)/shard_map/all_to_all | solution.py:47
  143.1 13.4 %fusion.9 = f32[12,256,256]{2,0,1:T(8,128)} fusion(f32[16,2,256,256]{3,1,2,0:T(2,128)} %all-to-all-done, f32[12,16,2]{1,2,0:T(2,128)S(1)} %convert_reduce_fusion), kind=kOutput, calls=%fused_computation.22 | convolution fusion | flops 301989888 | bytes 11535872 | tf_op jit(solution)/shard_map/msj,sjab->mab/dot_general | solution.py:58
  156.5 4.9 copy.64
  161.3 4.1 broadcast_select_fusion.1
  165.5 181.0 %all-reduce.8.cloned.1.call-done = f32[12,256,256]{1,2,0:T(8,128)} async-done(((f32[12,256,256]{1,2,0:T(8,128)}), f32[12,256,256]{1,2,0:T(8,128)}) %all-reduce.8.cloned.1.call-update) | async-done | bytes 3145744 | tf_op jit(solution)/shard_map/psum | solution.py:11
  346.5 1.7 fusion.17
  349.0 3.5 copy.67
  352.5 128.7 %all-reduce.10.cloned.1.call-done = f32[256,256]{0,1:T(8,128)} async-done(((f32[256,256]{0,1:T(8,128)}), f32[256,256]{0,1:T(8,128)}) %all-reduce.10.cloned.1.call-update) | async-done | bytes 262160 | tf_op jit(solution)/shard_map/psum | solution.py:11
  484.0 11.7 cholesky.130
  495.8 9.8 custom-call.13
  507.8 11.7 cholesky.147
  522.2 1.7 fusion.23
  524.5 4.0 while.4
  527.2 1.3 bitcast_dynamic-update-slice_fusion.4
  529.2 20.7 %custom-call.14 = f32[2,128,128]{1,2,0:T(8,128)S(1)} custom-call(f32[2,128,128]{2,1,0:T(8,128)} %copy-done.8), custom_call_target="InvertDiagBlocksLowerTriangular" | custom-call | tf_op jit(solution)/shard_map/triangular_solve/custom-call.0 | solution.py:23
  549.9 3.1 fusion.14
  552.9 2.7 convolution_subtract_fusion.1
  555.6 1.6 fusion.29
  557.2 2.0 pad_maximum_fusion
  559.2 3.5 copy.68
  562.8 3.6 copy.69
  567.4 2.3 select_select_fusion.1
  569.7 1.7 copy-done
  572.2 136.1 %all-reduce.12.cloned.1.call-done = f32[256,256]{0,1:T(8,128)} async-done(((f32[256,256]{0,1:T(8,128)}), f32[256,256]{0,1:T(8,128)}) %all-reduce.12.cloned.1.call-update) | async-done | bytes 262160 | tf_op jit(solution)/shard_map/psum | solution.py:11
  708.3 10.2 broadcast_select_fusion
  718.6 181.2 %all-reduce.14.cloned.1.call-done = f32[12,256,256]{1,2,0:T(8,128)} async-done(((f32[12,256,256]{1,2,0:T(8,128)}), f32[12,256,256]{1,2,0:T(8,128)}) %all-reduce.14.cloned.1.call-update) | async-done | bytes 3145744 | tf_op jit(solution)/shard_map/psum | solution.py:11
  899.8 1.7 fusion.16
  902.0 2.4 copy.75
  904.4 129.5 %all-reduce.16.cloned.1.call-done = f32[256,256]{0,1:T(8,128)} async-done(((f32[256,256]{0,1:T(8,128)}), f32[256,256]{0,1:T(8,128)}) %all-reduce.16.cloned.1.call-update) | async-done | bytes 262160 | tf_op jit(solution)/shard_map/psum | solution.py:11
  1036.6 11.7 cholesky.164
  1048.4 9.8 custom-call.15
  1060.4 11.7 cholesky.181
  1074.5 1.7 fusion.22
  1076.3 3.8 while.5
  1080.7 20.6 %custom-call.16 = f32[2,128,128]{1,2,0:T(8,128)S(1)} custom-call(f32[2,128,128]{2,1,0:T(8,128)} %copy-done.7), custom_call_target="InvertDiagBlocksLowerTriangular" | custom-call | tf_op jit(solution)/shard_map/triangular_solve/custom-call.0 | solution.py:23
  1101.4 1.5 fusion.12
  1102.9 2.7 convolution_subtract_fusion
  1105.6 1.6 fusion.25
  1107.4 2.4 copy.76
  1109.7 3.6 copy.77
  1113.5 2.3 select_select_fusion
  1116.6 136.2 %all-reduce.18.cloned.1.call-done = f32[256,256]{0,1:T(8,128)} async-done(((f32[256,256]{0,1:T(8,128)}), f32[256,256]{0,1:T(8,128)}) %all-reduce.18.cloned.1.call-update) | async-done | bytes 262160 | tf_op jit(solution)/shard_map/psum | solution.py:11
  1252.8 6.0 fusion.7
  1258.8 3.5 copy.81
  (89 shorter events, 27.5 us)
Async XLA Ops:
  25.6 117.5 %all-to-all-start = ((f32[16,2,256,256]{3,1,2,0:T(2,128)}), f32[16,2,256,256]{3,1,2,0:T(2,128)}, u32[]{:S(2)}, u32[]{:S(2)}) async-start(f32[16,2,256,256]{3,1,2,0:T(2,128)} %copy.61), calls=%async_computation | async-start | bytes 16777216 | tf_op jit(solution)/shard_map/all_to_all | solution.py:47
  32.3 314.3 %all-reduce.8.cloned.1.call-start = ((), (), s32[]{:S(2)}) async-start(), calls=%async_computation.1 | async-start | bytes 6291456 | tf_op jit(solution)/shard_map/psum | solution.py:11
  32.3 2.4 copy-start.9
  32.3 3.1 copy-start.10
  165.4 315.8 %all-reduce.10.cloned.1.call-start = ((), (), s32[]{:S(2)}) async-start(), calls=%async_computation.2 | async-start | bytes 524288 | tf_op jit(solution)/shard_map/psum | solution.py:11
  348.2 360.1 %all-reduce.12.cloned.1.call-start = ((), (), s32[]{:S(2)}) async-start(), calls=%async_computation.3 | async-start | bytes 524288 | tf_op jit(solution)/shard_map/psum | solution.py:11
  483.3 0.7 copy-start.5
  519.5 2.6 copy-start.2
  528.5 0.6 copy-start.8
  549.8 3.1 copy-start.1
  569.7 1.7 copy-start
  572.2 327.7 %all-reduce.14.cloned.1.call-start = ((), (), s32[]{:S(2)}) async-start(), calls=%async_computation.4 | async-start | bytes 6291456 | tf_op jit(solution)/shard_map/psum | solution.py:11
  718.5 315.3 %all-reduce.16.cloned.1.call-start = ((), (), s32[]{:S(2)}) async-start(), calls=%async_computation.5 | async-start | bytes 524288 | tf_op jit(solution)/shard_map/psum | solution.py:11
  901.5 351.3 %all-reduce.18.cloned.1.call-start = ((), (), s32[]{:S(2)}) async-start(), calls=%async_computation.6 | async-start | bytes 524288 | tf_op jit(solution)/shard_map/psum | solution.py:11
  1035.9 0.7 copy-start.6
  1072.1 2.4 copy-start.3
  1080.1 0.7 copy-start.7
  1109.7 3.6 copy-start.4
Sparse Core Ops, SparseCore 0:
  165.5 180.9 all-reduce.7
  349.1 132.0 all-reduce.9
  572.3 135.9 all-reduce.11
  718.7 181.0 all-reduce.13
  902.3 131.5 all-reduce.15
  1116.7 136.0 all-reduce.17
where the time goes:
time: 1280 us; the launch traced here: 1270 us
  waiting for transfers between devices  1000 us (78%)
  other arithmetic  134 us (10%)
  local copies, waits for them, and re-layouts  55.7 us (4%)
  matrix products  54.8 us (4%)
  between operations  16.6 us (1%)
    psum x6, waiting for transfers between devices, spread(): return lax.psum(block, axis)  893 us
    all_to_all x1, waiting for transfers between devices, per_device(): lax.all_to_all(outgoing, ('sub', 'row'), split_axis=0, concat_axis=0, til...  108 us
    another operation x14, other arithmetic, per_device(): factor = jnp.linalg.cholesky(diag)  69.2 us
    another operation x7, other arithmetic, right_solve(): lax.linalg.triangular_solve(factor, stacked.reshape(-1, tile), left_side=...  47.5 us
  transfers between devices with their start and end apart: 7, of which 7 were waited for; matrix products, arithmetic and copies ran while one was open for 1% of the time, Pallas kernels for 0%

commit v1 on v0

--- a/solution.py
+++ b/solution.py
@@ -6,9 +6,14 @@
 CAP = 2
 
 
+def load_stops_all_up(row_data, device_axis):
+    then = lax.all_gather(row_data, axis_name=device_axis)
+    return jnp.sum(then, 0)
+
+
 def spread(block, axis, holder):
     block = jnp.where(lax.axis_index(axis) == holder, block, jnp.zeros_like(block))
-    return lax.psum(block, axis)
+    return load_stops_all_up(block, axis)
 
 
 def slot_ranks(tile_map, owners):

time: 1280 us -> 1810 us (1.41)
  waiting for transfers between devices: 1000 us -> 1470 us
  other arithmetic: 134 us -> 200 us
    all_gather x0 -> x6, waiting for transfers between devices: none -> 1360 us  [load_stops_all_up(): then = lax.all_gather(row_data, axis_name=device_axis)]
    psum x6 -> x0, waiting for transfers between devices: 893 us -> none  [spread(): return lax.psum(block, axis)]
    reduce_sum x0 -> x6, other arithmetic: none -> 48.8 us  [load_stops_all_up(): return jnp.sum(then, 0)]
  transfers between devices with their start and end apart: 7 -> 7, of which waited for: 7 -> 7; matrix products, arithmetic and copies ran while one was open for 1% -> 0% of each run, Pallas kernels for 0% -> 0%
where the time goes in v1:
time: 1810 us; the launch traced here: 1800 us
  waiting for transfers between devices  1470 us (81%)
  other arithmetic  200 us (11%)
  matrix products  56.4 us (3%)
  local copies, waits for them, and re-layouts  53.2 us (3%)
    all_gather x6, waiting for transfers between devices, load_stops_all_up(): then = lax.all_gather(row_data, axis_name=device_axis)  1360 us
    all_to_all x1, waiting for transfers between devices, per_device(): lax.all_to_all(outgoing, ('sub', 'row'), split_axis=0, concat_axis=0, til...  110 us
    another operation x14, other arithmetic, per_device(): factor = jnp.linalg.cholesky(diag)  71.1 us
    reduce_sum x6, other arithmetic, load_stops_all_up(): return jnp.sum(then, 0)  48.8 us
    another operation x7, other arithmetic, right_solve(): lax.linalg.triangular_solve(factor, stacked.reshape(-1, tile), left_side=...  48.4 us
  transfers between devices with their start and end apart: 7, of which 7 were waited for; matrix products, arithmetic and copies ran while one was open for 0% of the time, Pallas kernels for 0%

profile of v1, /device:TPU:6, one launch (start us, length us, event | category | flops | bytes accessed | tf_op | source)
XLA Modules:
  0.0 1800.6 jit_solution(16571866450314409746)
XLA Ops:
  8.1 7.7 fusion.5
  15.9 9.7 copy.56
  25.6 7.0 all-to-all-start
  33.4 109.9 %all-to-all-done = f32[16,2,256,256]{3,1,2,0:T(2,128)} async-done(((f32[16,2,256,256]{3,1,2,0:T(2,128)}), f32[16,2,256,256]{3,1,2,0:T(2,128)}, u32[]{:S(2)}, u32[]{:S(2)}) %all-to-all-start) | async-done | bytes 8388640 | tf_op jit(solution)/shard_map/all_to_all | solution.py:52
  143.3 15.8 broadcast_select_fusion.1
  159.1 3.5 copy.59
  162.7 602.6 %all-gather.17.cloned.1.call-done = f32[192,256,256]{2,1,0:T(8,128)} async-done(((f32[12,256,256]{2,1,0:T(8,128)}), f32[192,256,256]{2,1,0:T(8,128)}) %all-gather.17.cloned.1.call-update) | async-done | bytes 50331664 | tf_op jit(solution)/shard_map/all_gather | solution.py:10
  765.3 17.6 reduce_sum.84
  784.3 35.8 %all-gather.9.cloned.1.call-done = f32[16,256,256]{2,1,0:T(8,128)} async-done(((f32[1,256,256]{2,1,0:T(8,128)}), f32[16,256,256]{2,1,0:T(8,128)}) %all-gather.9.cloned.1.call-update) | async-done | bytes 4194320 | tf_op jit(solution)/shard_map/all_gather | solution.py:10
  820.1 2.5 reduce_sum.85
  825.1 11.7 cholesky.130
  836.9 9.8 custom-call.13
  848.8 11.7 cholesky.147
  865.0 6.3 while.4
  866.1 2.3 bitcast_dynamic-update-slice_fusion.4
  869.1 2.2 bitcast_dynamic-update-slice_fusion.4
  871.9 20.5 %custom-call.14 = f32[2,128,128]{1,2,0:T(8,128)S(1)} custom-call(f32[2,128,128]{2,1,0:T(8,128)} %copy-done.11), custom_call_target="InvertDiagBlocksLowerTriangular" | custom-call | tf_op jit(solution)/shard_map/triangular_solve/custom-call.0 | solution.py:28
  894.0 3.5 convolution_subtract_fusion.1
  899.1 2.0 pad_maximum_fusion
  901.1 2.4 copy.64
  903.4 2.1 fusion.8
  905.6 1.9 copy-done.4
  908.6 40.1 %all-gather.11.cloned.1.call-done = f32[16,256,256]{2,1,0:T(8,128)} async-done(((f32[1,256,256]{2,1,0:T(8,128)}), f32[16,256,256]{2,1,0:T(8,128)}) %all-gather.11.cloned.1.call-update) | async-done | bytes 4194320 | tf_op jit(solution)/shard_map/all_gather | solution.py:10
  948.6 3.2 reduce_sum.86
  951.8 6.6 fusion.12
  958.4 4.1 broadcast_select_fusion
  962.5 3.5 copy.69
  966.1 602.1 %all-gather.19.cloned.1.call-done = f32[192,256,256]{2,1,0:T(8,128)} async-done(((f32[12,256,256]{2,1,0:T(8,128)}), f32[192,256,256]{2,1,0:T(8,128)}) %all-gather.19.cloned.1.call-update) | async-done | bytes 50331664 | tf_op jit(solution)/shard_map/all_gather | solution.py:10
  1568.2 19.3 %reduce_sum.87 = f32[12,256,256]{2,1,0:T(8,128)} reduce(f32[16,12,256,256]{3,2,1,0:T(8,128)} %bitcast.133, f32[]{:T(128)} %constant.149.clone.1), dimensions={0}, to_apply=%region_10.13 | reduce | flops 11796480 | bytes 53477380 | tf_op jit(solution)/shard_map/reduce_sum | solution.py:11
  1590.2 35.3 %all-gather.13.cloned.1.call-done = f32[16,256,256]{2,1,0:T(8,128)} async-done(((f32[1,256,256]{2,1,0:T(8,128)}), f32[16,256,256]{2,1,0:T(8,128)}) %all-gather.13.cloned.1.call-update) | async-done | bytes 4194320 | tf_op jit(solution)/shard_map/all_gather | solution.py:10
  1625.5 3.2 reduce_sum.88
  1632.2 11.7 cholesky.164
  1645.2 9.8 custom-call.15
  1657.8 11.7 cholesky.181
  1675.2 7.8 while.5
  1677.0 2.4 bitcast_dynamic-update-slice_fusion.5
  1680.7 2.3 bitcast_dynamic-update-slice_fusion.5
  1683.7 20.5 %custom-call.16 = f32[2,128,128]{1,2,0:T(8,128)S(1)} custom-call(f32[2,128,128]{2,1,0:T(8,128)} %copy-done.12), custom_call_target="InvertDiagBlocksLowerTriangular" | custom-call | tf_op jit(solution)/shard_map/triangular_solve/custom-call.0 | solution.py:28
  1704.2 3.1 fusion.16
  1707.3 3.5 convolution_subtract_fusion
  1712.4 2.0 pad_maximum_fusion.1
  1714.4 3.6 copy.74
  1718.0 4.0 fusion.7
  1725.0 40.1 %all-gather.15.cloned.1.call-done = f32[16,256,256]{2,1,0:T(8,128)} async-done(((f32[1,256,256]{2,1,0:T(8,128)}), f32[16,256,256]{2,1,0:T(8,128)}) %all-gather.15.cloned.1.call-update) | async-done | bytes 4194320 | tf_op jit(solution)/shard_map/all_gather | solution.py:10
  1765.1 3.2 reduce_sum.89
  1768.3 6.6 fusion.10
  1774.9 15.2 fusion.4
  1790.1 3.5 copy.79
  (108 shorter events, 40.5 us)
Async XLA Ops:
  25.6 7.2 copy-start.13
  25.6 7.9 copy-start.15
  25.6 117.8 %copy-start.6 = (f32[12,1,256,256]{3,2,1,0:T(8,128)S(1)}, f32[12,1,256,256]{3,2,1,0:T(8,128)}, u32[]{:S(2)}) copy-start(f32[12,1,256,256]{3,2,1,0:T(8,128)} %param.7) | copy-start | bytes 9437188
  25.6 117.8 %all-to-all-start = ((f32[16,2,256,256]{3,1,2,0:T(2,128)}), f32[16,2,256,256]{3,1,2,0:T(2,128)}, u32[]{:S(2)}, u32[]{:S(2)}) async-start(f32[16,2,256,256]{3,1,2,0:T(2,128)} %copy.56), calls=%async_computation | async-start | bytes 16777216 | tf_op jit(solution)/shard_map/all_to_all | solution.py:52
  32.5 732.8 %all-gather.17.cloned.1.call-start = ((), (), s32[]{:S(2)}) async-start(), calls=%async_computation.5 | async-start | bytes 53477376 | tf_op jit(solution)/shard_map/all_gather | solution.py:10
  162.7 657.4 %all-gather.9.cloned.1.call-start = ((), (), s32[]{:S(2)}) async-start(), calls=%async_computation.1 | async-start | bytes 4456448 | tf_op jit(solution)/shard_map/all_gather | solution.py:10
  784.0 164.7 %all-gather.11.cloned.1.call-start = ((), (), s32[]{:S(2)}) async-start(), calls=%async_computation.2 | async-start | bytes 4456448 | tf_op jit(solution)/shard_map/all_gather | solution.py:10
  824.4 0.7 copy-start.9
  860.6 2.7 copy-start.8
  871.3 0.6 copy-start.11
  871.9 27.1 %copy-start.16 = (s32[2,2]{1,0:T(2,128)}, s32[2,2]{1,0:T(2,128)S(1)}, u32[]{:S(2)}) copy-start(s32[2,2]{1,0:T(2,128)S(1)} %get-tuple-element.184) | copy-start | bytes 52
  905.5 1.9 copy-start.4
  908.5 659.7 %all-gather.19.cloned.1.call-start = ((), (), s32[]{:S(2)}) async-start(), calls=%async_computation.6 | async-start | bytes 53477376 | tf_op jit(solution)/shard_map/all_gather | solution.py:10
  951.8 6.6 copy-start
  958.4 4.1 copy-start.2
  966.0 659.5 %all-gather.13.cloned.1.call-start = ((), (), s32[]{:S(2)}) async-start(), calls=%async_computation.3 | async-start | bytes 4456448 | tf_op jit(solution)/shard_map/all_gather | solution.py:10
  1589.4 175.7 %all-gather.15.cloned.1.call-start = ((), (), s32[]{:S(2)}) async-start(), calls=%async_computation.4 | async-start | bytes 4456448 | tf_op jit(solution)/shard_map/all_gather | solution.py:10
  1631.5 0.7 copy-start.10
  1683.1 0.7 copy-start.12
  1704.2 3.1 copy-start.5
  1714.4 3.6 copy-start.14
  1722.0 1.9 copy-start.3
  1768.3 6.6 copy-start.1
  1768.3 6.6 copy-start.7
Sparse Core Ops, SparseCore 0:
  162.8 602.5 all-gather.16
  784.1 35.9 all-gather.8
  908.6 39.9 all-gather.10
  966.2 601.9 all-gather.18
  1589.5 35.9 all-gather.12
  1725.1 39.9 all-gather.14
